TPU v7x, 256 devices: a whole 4x4x8 slice. The times are simulated.
256 devices in a mesh: section: 8 (over x, z_hi), dp: 4 (over y), expert: 8 (over z_lo, core).
Axes of the slice: x: 4, y: 4, z: 8 (z_hi: 2, z_lo: 4; z = z_hi * 4 + z_lo), core: 2. Of those that a mesh axis runs over, the one named last changes fastest.
Arguments:
- tokens: bfloat16 [8, 4096, 2560], P('section', ('dp', 'expert')), may hold values from -6 to 6
- cotangent: bfloat16 [8, 4096, 2560], P('section', ('dp', 'expert')), may hold values from -3 to 3
- routes: int32 [8, 4096, 6], P('section', ('dp', 'expert')), may hold values from 0 to 159, as said below
- gates: float32 [8, 4096, 6], P('section', ('dp', 'expert')), may hold values from 0.2 to 1
- gate_up: bfloat16 [8, 8, 2, 1024, 2560], P('section', 'expert', None, 'dp'), may hold values from -0.125 to 0.125
- down: bfloat16 [8, 8, 1024, 2560], P('section', 'expert', 'dp'), may hold values from -0.1875 to 0.1875
Outputs:
- handed_on: bfloat16 [8, 4096, 2560], P('section', ('dp', 'expert'))
- handed_back: bfloat16 [8, 4096, 2560], P('section', ('dp', 'expert'))
- grad_gate_up: bfloat16 [8, 8, 2, 1024, 2560], P('section', 'expert', None, 'dp')
- grad_down: bfloat16 [8, 8, 1024, 2560], P('section', 'expert', 'dp')
Inputs may be any that keep to these rules, and one draw needn't show every extreme that they name: `routes`: A token's 6 ids are distinct and at most one of them is below 8. In each device's block of 128 tokens no id below 8 is named by more than 16 tokens.
All inputs are finite; a program needn't handle non-finite values.
Results may differ from a plain program's by a relative error of at most 0.0065.
Values may be sent and summed in bfloat16 or wider, within the bound.
A program may use at most 64 MiB of HBM per device.

v0:
```python
import jax
import jax.numpy as jnp
from jax import lax
from jax.sharding import PartitionSpec as P


def joined_along(parts, dim):
    dims = list(parts.shape[1:])
    dims[dim] *= parts.shape[0]
    return jnp.moveaxis(parts, 0, dim).reshape(dims)


def copy_for_each(value, axis):
    copies = jnp.broadcast_to(value, (lax.axis_size(axis), *value.shape))
    return lax.all_to_all(copies, axis, split_axis=0, concat_axis=0, tiled=True)


def gather_directly(value, axis, dim):
    return joined_along(copy_for_each(value, axis), dim)


def passed_along(value, axis, steps):
    count = lax.axis_size(axis)
    first, last = (max(0, -steps), min(count, count - steps))
    return lax.ppermute(value, axis, [(source, source + steps) for source in range(first, last)])


def to_experts(buffer):
    columns = lax.all_to_all(buffer, "expert", split_axis=0, concat_axis=0, tiled=True)
    arrived = gather_directly(columns, "dp", 0)
    return arrived


def to_owners(partial_value):
    copies = lax.axis_size("dp")
    quarters = lax.all_to_all(partial_value, "dp", split_axis=0, concat_axis=0, tiled=True)
    quarters = quarters.reshape((copies, quarters.shape[0] // copies) + quarters.shape[1:])
    column_rows = jnp.sum(quarters.astype(jnp.float32), 0).astype(jnp.bfloat16)
    summed = lax.all_to_all(column_rows, "expert", split_axis=0, concat_axis=0, tiled=True)
    return summed


def shards(tokens, cotangent, routes, gates, gate_up, down):
    window = lax.axis_size("expert")
    copies = lax.axis_size("dp")
    rows_here = tokens.shape[1]
    model_width = tokens.shape[2]
    capacity = rows_here // window
    in_window = routes[0] < window
    expert_of = jnp.sum(jnp.where(in_window, routes[0], 0), -1)
    present = jnp.any(in_window, -1)
    weight = jnp.sum(jnp.where(in_window, gates[0], 0.0), -1)
    member = ((expert_of[:, None] == jnp.arange(window)[None, :]) & present[:, None]).astype(
        jnp.float32
    )
    before = jnp.cumsum(member, 0) - member
    slot_index = jnp.sum(before * member, -1)
    slot_values = jnp.arange(capacity, dtype=jnp.float32)
    select = member.T[:, None, :] * (slot_index[None, None, :] == slot_values[None, :, None])
    select = select.astype(jnp.bfloat16).reshape(window * capacity, rows_here)
    contract_last = (((1,), (1,)), ((), ()))
    contract_first = (((0,), (0,)), ((), ()))

    def to_slots(values):
        packed = jnp.dot(select, values, preferred_element_type=jnp.float32).astype(jnp.bfloat16)
        arrived = to_experts(packed.reshape(window, capacity, model_width))
        return arrived.reshape(copies * window * capacity, model_width)

    def from_slots(partial_value):
        rounded = partial_value.astype(jnp.bfloat16).reshape(copies * window, capacity, model_width)
        owner_rows = to_owners(rounded).reshape(window * capacity, model_width)
        return lax.dot_general(
            select, owner_rows, contract_first, preferred_element_type=jnp.float32
        )

    gate_matrix = gate_up[0, 0, 0]
    up_matrix = gate_up[0, 0, 1]
    down_matrix = down[0, 0]
    slot_rows = to_slots(tokens[0])
    pre_gate = lax.dot_general(
        slot_rows, gate_matrix, contract_last, preferred_element_type=jnp.float32
    )
    pre_up = lax.dot_general(
        slot_rows, up_matrix, contract_last, preferred_element_type=jnp.float32
    )
    sigmoid_gate = jax.nn.sigmoid(pre_gate)
    activated = pre_gate * sigmoid_gate
    hidden = (activated * pre_up).astype(jnp.bfloat16)
    partial_value = jnp.dot(hidden, down_matrix, preferred_element_type=jnp.float32)
    mixture = (from_slots(partial_value) * weight[:, None]).astype(jnp.bfloat16)
    handed_on = passed_along(mixture[None], "section", 1)
    scaled = (cotangent[0].astype(jnp.float32) * weight[:, None]).astype(jnp.bfloat16)
    slot_grads = to_slots(scaled)
    hidden_grad = lax.dot_general(
        slot_grads, down_matrix, contract_last, preferred_element_type=jnp.float32
    )
    grad_down = lax.dot_general(
        hidden, slot_grads, contract_first, preferred_element_type=jnp.float32
    ).astype(jnp.bfloat16)
    gate_slope = sigmoid_gate * (1.0 + pre_gate * (1.0 - sigmoid_gate))
    gate_grad = (hidden_grad * pre_up * gate_slope).astype(jnp.bfloat16)
    up_grad = (hidden_grad * activated).astype(jnp.bfloat16)
    grad_gate = lax.dot_general(
        gate_grad, slot_rows, contract_first, preferred_element_type=jnp.float32
    ).astype(jnp.bfloat16)
    grad_up = lax.dot_general(
        up_grad, slot_rows, contract_first, preferred_element_type=jnp.float32
    ).astype(jnp.bfloat16)
    input_part = jnp.dot(gate_grad, gate_matrix, preferred_element_type=jnp.float32)
    input_part = input_part + jnp.dot(up_grad, up_matrix, preferred_element_type=jnp.float32)
    input_grad = from_slots(input_part).astype(jnp.bfloat16)
    handed_back = passed_along(input_grad[None], "section", -1)
    grads_pair = jnp.stack([grad_gate, grad_up])[None, None]
    return (handed_on, handed_back, grads_pair, grad_down[None, None])


def solution(mesh):
    in_specs = (
        P("section", ("dp", "expert"), None),
        P("section", ("dp", "expert"), None),
        P("section", ("dp", "expert"), None),
        P("section", ("dp", "expert"), None),
        P("section", "expert", None, "dp", None),
        P("section", "expert", "dp", None),
    )
    out_specs = (
        P("section", ("dp", "expert"), None),
        P("section", ("dp", "expert"), None),
        P("section", "expert", None, "dp", None),
        P("section", "expert", "dp", None),
    )
    return jax.shard_map(shards, mesh=mesh, in_specs=in_specs, out_specs=out_specs, check_vma=False)
```

profile of v0, /device:TPU:4, one launch (start us, length us, event | category | flops | bytes accessed | tf_op | source)
XLA Modules:
  0.0 330.3 jit_solution(8226063930759521639)
XLA Ops:
  0.6 0.0 copy-start
  0.6 0.0 copy-start.6
  0.7 0.8 fusion.31
  1.5 0.7 fusion.34
  2.2 0.1 fusion.28
  2.3 0.7 fusion.30
  3.0 0.2 reduce_window_sum.11
  3.2 0.2 select_reduce_fusion
  3.4 2.3 convolution_convert_fusion.4
  5.7 5.9 %all-to-all-start.4 = ((bf16[8,16,2560]{2,1,0:T(8,128)(2,1)}), bf16[8,16,2560]{2,1,0:T(8,128)(2,1)S(1)}, u32[]{:S(2)}, u32[]{:S(2)}) async-start(bf16[8,16,2560]{2,1,0:T(8,128)(2,1)} %bitcast.12), calls=%async_computation.4 | async-start | bytes 1310720 | tf_op jit(solution)/shard_map/all_to_all | solution.py:29
  11.6 0.0 copy-done.6
  11.6 0.3 convolution_convert_fusion.5
  12.0 17.8 %all-to-all-done.4 = bf16[8,16,2560]{2,1,0:T(8,128)(2,1)S(1)} async-done(((bf16[8,16,2560]{2,1,0:T(8,128)(2,1)}), bf16[8,16,2560]{2,1,0:T(8,128)(2,1)S(1)}, u32[]{:S(2)}, u32[]{:S(2)}) %all-to-all-start.4) | async-done | bytes 655392 | tf_op jit(solution)/shard_map/all_to_all | solution.py:29
  29.8 20.5 %all_to_all.40 = bf16[8,16,2560]{2,1,0:T(8,128)(2,1)S(1)} all-to-all(bf16[8,16,2560]{2,1,0:T(8,128)(2,1)S(1)} %bitcast.95), channel_id=1, replica_groups=mesh['section'=8,'dp'=4,'expert'=8] {'expert'}, dimensions={0} | all-to-all | bytes 1310720 | tf_op jit(solution)/shard_map/all_to_all | solution.py:29
  50.4 0.3 broadcast_in_dim.35
  50.7 36.1 %all_to_all.41 = bf16[4,8,16,2560]{3,2,1,0:T(8,128)(2,1)} all-to-all(bf16[4,8,16,2560]{3,2,1,0:T(8,128)(2,1)S(1)} %broadcast_in_dim.35), channel_id=1, replica_groups=mesh['section'=8,'dp'=4,'expert'=8] {'dp'}, dimensions={0} | all-to-all | bytes 5242880 | tf_op jit(solution)/shard_map/all_to_all | solution.py:15
  86.8 1.8 broadcast_in_dim.38
  88.6 4.5 %all-to-all-start.5 = ((bf16[4,8,16,2560]{3,2,1,0:T(8,128)(2,1)}), bf16[4,8,16,2560]{3,2,1,0:T(8,128)(2,1)}, u32[]{:S(2)}, u32[]{:S(2)}) async-start(bf16[4,8,16,2560]{3,2,1,0:T(8,128)(2,1)} %broadcast_in_dim.38), calls=%async_computation.5 | async-start | bytes 5242880 | tf_op jit(solution)/shard_map/all_to_all | solution.py:15
  93.2 0.0 copy-start.1
  93.2 0.0 copy-start.3
  93.2 3.1 fusion.12
  96.3 0.0 copy-done.1
  96.3 0.5 copy-done.3
  96.9 0.9 fusion.16
  97.8 26.3 %all-to-all-done.5 = bf16[4,8,16,2560]{3,2,1,0:T(8,128)(2,1)} async-done(((bf16[4,8,16,2560]{3,2,1,0:T(8,128)(2,1)}), bf16[4,8,16,2560]{3,2,1,0:T(8,128)(2,1)}, u32[]{:S(2)}, u32[]{:S(2)}) %all-to-all-start.5) | async-done | bytes 2621472 | tf_op jit(solution)/shard_map/all_to_all | solution.py:15
  124.1 0.0 copy-done
  124.1 2.7 multiply_convert_fusion.1
  126.8 0.0 copy-start.5
  126.8 2.3 convolution_convert_fusion
  129.1 4.6 %all-to-all-start.2 = ((bf16[32,16,2560]{2,1,0:T(8,128)(2,1)}), bf16[32,16,2560]{2,1,0:T(8,128)(2,1)}, u32[]{:S(2)}, u32[]{:S(2)}) async-start(bf16[32,16,2560]{2,1,0:T(8,128)(2,1)} %bitcast.93), calls=%async_computation.2 | async-start | bytes 5242880 | tf_op jit(solution)/shard_map/all_to_all | solution.py:36
  133.7 0.0 copy-start.4
  133.7 2.3 fusion.14
  136.0 0.0 copy-done.5
  136.0 0.0 copy-done.4
  136.0 2.4 add_convert_fusion
  138.4 25.3 %all-to-all-done.2 = bf16[32,16,2560]{2,1,0:T(8,128)(2,1)} async-done(((bf16[32,16,2560]{2,1,0:T(8,128)(2,1)}), bf16[32,16,2560]{2,1,0:T(8,128)(2,1)}, u32[]{:S(2)}, u32[]{:S(2)}) %all-to-all-start.2) | async-done | bytes 2621472 | tf_op jit(solution)/shard_map/all_to_all | solution.py:36
  163.7 4.6 %all-to-all-start.6 = ((bf16[32,16,2560]{2,1,0:T(8,128)(2,1)}), bf16[32,16,2560]{2,1,0:T(8,128)(2,1)}, u32[]{:S(2)}, u32[]{:S(2)}) async-start(bf16[32,16,2560]{2,1,0:T(8,128)(2,1)} %bitcast.94), calls=%async_computation.6 | async-start | bytes 5242880 | tf_op jit(solution)/shard_map/all_to_all | solution.py:36
  168.3 3.1 reduce_sum.53
  171.4 25.9 %all-to-all-done.6 = bf16[32,16,2560]{2,1,0:T(8,128)(2,1)} async-done(((bf16[32,16,2560]{2,1,0:T(8,128)(2,1)}), bf16[32,16,2560]{2,1,0:T(8,128)(2,1)}, u32[]{:S(2)}, u32[]{:S(2)}) %all-to-all-start.6) | async-done | bytes 2621472 | tf_op jit(solution)/shard_map/all_to_all | solution.py:36
  197.3 3.5 %all-to-all-start.3 = ((bf16[8,16,2560]{2,1,0:T(8,128)(2,1)}), bf16[8,16,2560]{2,1,0:T(8,128)(2,1)S(1)}, u32[]{:S(2)}, u32[]{:S(2)}) async-start(bf16[8,16,2560]{2,1,0:T(8,128)(2,1)} %reduce_sum.53), calls=%async_computation.3 | async-start | bytes 1310720 | tf_op jit(solution)/shard_map/all_to_all | solution.py:39
  200.9 3.1 reduce_sum.55
  204.0 14.9 %all-to-all-done.3 = bf16[8,16,2560]{2,1,0:T(8,128)(2,1)S(1)} async-done(((bf16[8,16,2560]{2,1,0:T(8,128)(2,1)}), bf16[8,16,2560]{2,1,0:T(8,128)(2,1)S(1)}, u32[]{:S(2)}, u32[]{:S(2)}) %all-to-all-start.3) | async-done | bytes 655392 | tf_op jit(solution)/shard_map/all_to_all | solution.py:39
  219.0 4.2 %all-to-all-start.7 = ((bf16[8,16,2560]{2,1,0:T(8,128)(2,1)}), bf16[8,16,2560]{2,1,0:T(8,128)(2,1)}, u32[]{:S(2)}, u32[]{:S(2)}) async-start(bf16[8,16,2560]{2,1,0:T(8,128)(2,1)} %reduce_sum.55), calls=%async_computation.7 | async-start | bytes 1310720 | tf_op jit(solution)/shard_map/all_to_all | solution.py:39
  223.2 0.0 copy-start.2
  223.2 3.8 %fusion.2 = bf16[1,1,256,2560]{3,2,1,0:T(8,128)(2,1)} fusion(bf16[512,256]{1,0:T(8,128)(2,1)S(1)} %get-tuple-element.6, bf16[512,2560]{1,0:T(8,128)(2,1)} %bitcast.13), kind=kOutput, calls=%fused_computation.7 | convolution fusion | flops 671744000 | bytes 4194304 | tf_op jit(solution)/shard_map/dot_general | solution.py:97
  227.0 0.0 copy-done.2
  227.0 1.8 fusion.1
  228.8 1.2 fusion.6
  230.0 6.7 %collective-permute-start = (bf16[1,128,2560]{2,1,0:T(8,128)(2,1)}, bf16[1,128,2560]{2,1,0:T(8,128)(2,1)}, u32[]{:S(2)}, u32[]{:S(2)}) collective-permute-start(bf16[1,128,2560]{2,1,0:T(8,128)(2,1)} %fusion.6), channel_id=1, source_target_pairs={{0,32},{32,64},{64,96},{96,128},{128,160},{160,192},{192,224},{1,3... | collective-permute-start | bytes 1966088 | tf_op jit(solution)/shard_map/ppermute | solution.py:25
  236.7 53.9 %all-to-all-done.7 = bf16[8,16,2560]{2,1,0:T(8,128)(2,1)} async-done(((bf16[8,16,2560]{2,1,0:T(8,128)(2,1)}), bf16[8,16,2560]{2,1,0:T(8,128)(2,1)}, u32[]{:S(2)}, u32[]{:S(2)}) %all-to-all-start.7) | async-done | bytes 655392 | tf_op jit(solution)/shard_map/all_to_all | solution.py:39
  290.6 1.4 fusion.7
  292.0 10.0 %collective-permute-start.1 = (bf16[1,128,2560]{2,1,0:T(8,128)(2,1)S(1)}, bf16[1,128,2560]{2,1,0:T(8,128)(2,1)S(1)}, u32[]{:S(2)}, u32[]{:S(2)}) collective-permute-start(bf16[1,128,2560]{2,1,0:T(8,128)(2,1)S(1)} %fusion.7), channel_id=1, source_target_pairs={{32,0},{64,32},{96,64},{128,96},{160,128},{192,160},{224,192},{33,... | collective-permute-start | bytes 1966088 | tf_op jit(solution)/shard_map/ppermute | solution.py:25
  302.1 2.6 fusion
  304.7 1.7 maximum_bitcast_fusion
  306.4 0.0 collective-permute-done
  306.4 21.1 %collective-permute-done.1 = bf16[1,128,2560]{2,1,0:T(8,128)(2,1)S(1)} collective-permute-done((bf16[1,128,2560]{2,1,0:T(8,128)(2,1)S(1)}, bf16[1,128,2560]{2,1,0:T(8,128)(2,1)S(1)}, u32[]{:S(2)}, u32[]{:S(2)}) %collective-permute-start.1) | collective-permute-done | bytes 655392 | tf_op jit(solution)/shard_map/ppermute | solution.py:25
  327.5 2.0 copy.25
  329.5 0.8 copy.26
  (3 shorter events, 0.0 us)
Async XLA Ops:
  0.6 123.4 %copy-start = (bf16[1,1,256,2560]{3,2,1,0:T(8,128)(2,1)S(1)}, bf16[1,1,256,2560]{3,2,1,0:T(8,128)(2,1)}, u32[]{:S(2)}) copy-start(bf16[1,1,256,2560]{3,2,1,0:T(8,128)(2,1)} %param.11) | copy-start | bytes 3932164
  0.6 11.0 %copy-start.6 = (bf16[1,128,2560]{2,1,0:T(8,128)(2,1)S(1)}, bf16[1,128,2560]{2,1,0:T(8,128)(2,1)}, u32[]{:S(2)}) copy-start(bf16[1,128,2560]{2,1,0:T(8,128)(2,1)} %param.6) | copy-start | bytes 1966084
  5.7 24.1 %all-to-all-start.4 = ((bf16[8,16,2560]{2,1,0:T(8,128)(2,1)}), bf16[8,16,2560]{2,1,0:T(8,128)(2,1)S(1)}, u32[]{:S(2)}, u32[]{:S(2)}) async-start(bf16[8,16,2560]{2,1,0:T(8,128)(2,1)} %bitcast.12), calls=%async_computation.4 | async-start | bytes 1310720 | tf_op jit(solution)/shard_map/all_to_all | solution.py:29
  88.6 35.4 %all-to-all-start.5 = ((bf16[4,8,16,2560]{3,2,1,0:T(8,128)(2,1)}), bf16[4,8,16,2560]{3,2,1,0:T(8,128)(2,1)}, u32[]{:S(2)}, u32[]{:S(2)}) async-start(bf16[4,8,16,2560]{3,2,1,0:T(8,128)(2,1)} %broadcast_in_dim.38), calls=%async_computation.5 | async-start | bytes 5242880 | tf_op jit(solution)/shard_map/all_to_all | solution.py:15
  93.2 3.2 copy-start.1
  93.2 3.7 %copy-start.3 = (bf16[1,1,2,256,2560]{4,3,2,1,0:T(8,128)(2,1)S(1)}, bf16[1,1,2,256,2560]{4,3,2,1,0:T(8,128)(2,1)}, u32[]{:S(2)}) copy-start(bf16[1,1,2,256,2560]{4,3,2,1,0:T(8,128)(2,1)} %param.10) | copy-start | bytes 7864324
  126.8 9.3 %copy-start.5 = (bf16[512,256]{1,0:T(8,128)(2,1)}, bf16[512,256]{1,0:T(8,128)(2,1)S(1)}, u32[]{:S(2)}) copy-start(bf16[512,256]{1,0:T(8,128)(2,1)S(1)} %get-tuple-element.4) | copy-start | bytes 786436
  129.1 34.5 %all-to-all-start.2 = ((bf16[32,16,2560]{2,1,0:T(8,128)(2,1)}), bf16[32,16,2560]{2,1,0:T(8,128)(2,1)}, u32[]{:S(2)}, u32[]{:S(2)}) async-start(bf16[32,16,2560]{2,1,0:T(8,128)(2,1)} %bitcast.93), calls=%async_computation.2 | async-start | bytes 5242880 | tf_op jit(solution)/shard_map/all_to_all | solution.py:36
  133.7 2.3 copy-start.4
  163.7 33.7 %all-to-all-start.6 = ((bf16[32,16,2560]{2,1,0:T(8,128)(2,1)}), bf16[32,16,2560]{2,1,0:T(8,128)(2,1)}, u32[]{:S(2)}, u32[]{:S(2)}) async-start(bf16[32,16,2560]{2,1,0:T(8,128)(2,1)} %bitcast.94), calls=%async_computation.6 | async-start | bytes 5242880 | tf_op jit(solution)/shard_map/all_to_all | solution.py:36
  197.3 21.6 %all-to-all-start.3 = ((bf16[8,16,2560]{2,1,0:T(8,128)(2,1)}), bf16[8,16,2560]{2,1,0:T(8,128)(2,1)S(1)}, u32[]{:S(2)}, u32[]{:S(2)}) async-start(bf16[8,16,2560]{2,1,0:T(8,128)(2,1)} %reduce_sum.53), calls=%async_computation.3 | async-start | bytes 1310720 | tf_op jit(solution)/shard_map/all_to_all | solution.py:39
  219.0 71.6 %all-to-all-start.7 = ((bf16[8,16,2560]{2,1,0:T(8,128)(2,1)}), bf16[8,16,2560]{2,1,0:T(8,128)(2,1)}, u32[]{:S(2)}, u32[]{:S(2)}) async-start(bf16[8,16,2560]{2,1,0:T(8,128)(2,1)} %reduce_sum.55), calls=%async_computation.7 | async-start | bytes 1310720 | tf_op jit(solution)/shard_map/all_to_all | solution.py:39
  223.2 3.8 %copy-start.2 = (bf16[4,8,16,2560]{3,2,1,0:T(8,128)(2,1)S(1)}, bf16[4,8,16,2560]{3,2,1,0:T(8,128)(2,1)}, u32[]{:S(2)}) copy-start(bf16[4,8,16,2560]{3,2,1,0:T(8,128)(2,1)} %all_to_all.41) | copy-start | bytes 7864324
  230.0 76.4 %collective-permute-start = (bf16[1,128,2560]{2,1,0:T(8,128)(2,1)}, bf16[1,128,2560]{2,1,0:T(8,128)(2,1)}, u32[]{:S(2)}, u32[]{:S(2)}) collective-permute-start(bf16[1,128,2560]{2,1,0:T(8,128)(2,1)} %fusion.6), channel_id=1, source_target_pairs={{0,32},{32,64},{64,96},{96,128},{128,160},{160,192},{192,224},{1,3... | collective-permute-start | bytes 1966088 | tf_op jit(solution)/shard_map/ppermute | solution.py:25
  292.0 35.5 %collective-permute-start.1 = (bf16[1,128,2560]{2,1,0:T(8,128)(2,1)S(1)}, bf16[1,128,2560]{2,1,0:T(8,128)(2,1)S(1)}, u32[]{:S(2)}, u32[]{:S(2)}) collective-permute-start(bf16[1,128,2560]{2,1,0:T(8,128)(2,1)S(1)} %fusion.7), channel_id=1, source_target_pairs={{32,0},{64,32},{96,64},{128,96},{160,128},{192,160},{224,192},{33,... | collective-permute-start | bytes 1966088 | tf_op jit(solution)/shard_map/ppermute | solution.py:25
where the time goes:
time: 331 us; the launch traced here: 330 us
  waiting for transfers between devices  185 us (56%)
  blocking collectives  56.7 us (17%)
  starting transfers between devices  44 us (13%)
  matrix products  27.2 us (8%)
  other arithmetic  10.8 us (3%)
  local copies, waits for them, and re-layouts  5.49 us (2%)
    all_to_all x2, waiting for transfers between devices, to_owners(): lax.all_to_all(column_rows, 'expert', split_axis=0, concat_axis=0, tiled=...  68.9 us
    all_to_all x2, waiting for transfers between devices, to_owners(): lax.all_to_all(partial_value, 'dp', split_axis=0, concat_axis=0, tiled=True)  51.2 us
    all_to_all x1, blocking collectives, copy_for_each(): return lax.all_to_all(copies, axis, split_axis=0, concat_axis=0, tiled=True)  36.1 us
    all_to_all x1, waiting for transfers between devices, copy_for_each(): return lax.all_to_all(copies, axis, split_axis=0, concat_axis=0, tiled=True)  26.3 us
    ppermute x2, waiting for transfers between devices, passed_along(): lax.ppermute(value, axis, [(source, source + steps) for source in range(f...  21.1 us
    all_to_all x1, blocking collectives, to_experts(): lax.all_to_all(buffer, 'expert', split_axis=0, concat_axis=0, tiled=True)  20.5 us
    all_to_all x1, waiting for transfers between devices, to_experts(): lax.all_to_all(buffer, 'expert', split_axis=0, concat_axis=0, tiled=True)  17.8 us
    ppermute x2, starting transfers between devices, passed_along(): lax.ppermute(value, axis, [(source, source + steps) for source in range(f...  16.7 us
  transfers between devices with their start and end apart: 8, of which 7 were waited for; matrix products, arithmetic and copies ran while one was open for 8% of the time, Pallas kernels for 0%

commit v1 on v0

v1 whole, which is shorter than its diff:
```python
import functools

import jax
import jax.numpy as jnp
from jax import lax
from jax.experimental import pallas as pl
from jax.experimental.pallas import tpu as pltpu
from jax.sharding import PartitionSpec as P

MESH = pl.DeviceIdType.MESH
F32 = jnp.float32
BF16 = jnp.bfloat16
NT = (((1,), (1,)), ((), ()))
COLS = 512
COPIES = 80


def flipped(index, bits):
    out = index
    for b in range(3):
        if bits >> b & 1:
            out = out + (1 << b) * (1 - 2 * ((index // (1 << b)) % 2))
    return out


def kernel(
    tok_hbm, cot_hbm, routes_ref, gates_ref, gu_hbm, dn_hbm,
    on_hbm, back_hbm, ggu_hbm, gdn_hbm,
    tok, cot, wgu, wdn, pk, xs, part, rdiag, rown, fin, rsec, metas, metar,
    act, bsl, hid_t, gr_t, ggu, gdn, outs, lsem, osem, ssem, rsem,
):
    s = lax.axis_index("section")
    q = lax.axis_index("dp")
    e = lax.axis_index("expert")
    nxt, prv = (s + 1) % 8, (s + 7) % 8
    up, dwn = (q + 1) % 4, (q + 3) % 4
    rows, width = tok.shape
    n_tiles = width // COLS

    barrier = pltpu.get_barrier_semaphore()
    peers = [(s, q, flipped(e, k)) for k in range(1, 8)]
    peers += [(s, up, e), (s, dwn, e)]
    peers += [(t, q, flipped(e, k)) for t in (nxt, prv) for k in range(8)]
    for peer in peers:
        pl.semaphore_signal(barrier, inc=1, device_id=peer, device_id_type=MESH)

    loads = [
        pltpu.make_async_copy(src, dst, lsem.at[i])
        for i, (src, dst) in enumerate(
            ((tok_hbm, tok), (cot_hbm, cot), (gu_hbm, wgu), (dn_hbm, wdn))
        )
    ]
    for load in loads:
        load.start()

    used = []

    def copy(src, dst, peer):
        i = len(used)
        c = pltpu.make_async_remote_copy(
            src_ref=src, dst_ref=dst, send_sem=ssem.at[i], recv_sem=rsem.at[i],
            device_id=peer, device_id_type=MESH,
        )
        used.append(c)
        return c

    def tiles(body):
        @pl.loop(0, n_tiles)
        def _(j):
            body(pl.ds(pl.multiple_of(j * COLS, COLS), COLS))

    def chunk(ref, t, r, c):
        return ref.at[t, pl.ds(r * rows + c * 32, 32)]

    sides = ((up, 3), (dwn, 1))
    zc = [
        [None] + [
            copy(pk.at[t, pl.ds(k * 16, 16)], xs.at[t, pl.ds(k * 16, 16)], (s, q, flipped(e, k)))
            for k in range(1, 8)
        ]
        for t in range(2)
    ]
    own = [
        [[copy(chunk(xs, t, 0, c), chunk(xs, t, r, c), (s, y, e)) for y, r in sides] for c in range(4)]
        for t in range(2)
    ]
    onward = [
        [
            copy(chunk(xs, t, 3, c), chunk(xs, t, 2, c), (s, up, e)) if c < 2
            else copy(chunk(xs, t, 1, c), chunk(xs, t, 2, c), (s, dwn, e))
            for c in range(4)
        ]
        for t in range(2)
    ]
    far = [
        [
            copy(chunk(part, t, 2, c), rdiag.at[t, pl.ds(c * 32, 32)], (s, (up, dwn)[c // 2], e))
            for c in range(4)
        ]
        for t in range(2)
    ]
    near = [
        [
            [
                copy(chunk(part, t, r, c), rown.at[t, side, pl.ds(c * 32, 32)], (s, y, e))
                for side, (y, r) in enumerate(((up, 1), (dwn, 3)))
            ]
            for c in range(4)
        ]
        for t in range(2)
    ]
    final = [
        [
            copy(fin.at[t, pl.ds(k * 16, 16)], rsec.at[t, pl.ds(k * 16, 16)], ((nxt, prv)[t], q, flipped(e, k)))
            for k in range(8)
        ]
        for t in range(2)
    ]
    meta = [copy(metas, metar.at[t], ((nxt, prv)[t], q, e)) for t in range(2)]
    assert len(used) == COPIES

    in_window = routes_ref[...] < 8
    expert_of = jnp.sum(jnp.where(in_window, routes_ref[...].astype(F32), 0.0), 1, keepdims=True)
    present = jnp.sum(jnp.where(in_window, 1.0, 0.0), 1, keepdims=True) > 0.5
    weight = jnp.sum(jnp.where(in_window, gates_ref[...], 0.0), 1, keepdims=True)
    lane = lax.broadcasted_iota(jnp.int32, (rows, rows), 1)
    sub = lax.broadcasted_iota(jnp.int32, (rows, rows), 0)
    member = jnp.where((expert_of == lane.astype(F32)) & present, 1.0, 0.0)
    earlier = jnp.where(lane < sub, 1.0, 0.0).astype(BF16)
    before = jnp.dot(earlier, member.astype(BF16), preferred_element_type=F32)
    slot = jnp.sum(before * member, 1, keepdims=True)
    column = expert_of.astype(jnp.int32) ^ e
    place = jnp.where(present, column.astype(F32) * 16.0 + slot, -1.0)
    place_t = jnp.broadcast_to(place, (rows, rows)).T
    metas[0:8, :] = place_t[0:8, :]
    metas[8:16, :] = jnp.broadcast_to(weight, (rows, rows)).T[0:8, :]
    select = jnp.where(place_t == sub.astype(F32), 1.0, 0.0).astype(BF16)

    loads[0].wait()

    @tiles
    def _(cols):
        packed = jnp.dot(select, tok[:, cols], preferred_element_type=F32).astype(BF16)
        pk[0, :, cols] = packed
        xs[0, 0:16, cols] = packed[0:16, :]

    pl.semaphore_wait(barrier, len(peers))
    for k in (2, 3, 4, 5, 6, 7, 1):
        zc[0][k].start()

    loads[1].wait()

    @tiles
    def _(cols):
        scaled = (cot[:, cols].astype(F32) * weight).astype(BF16)
        packed = jnp.dot(select, scaled, preferred_element_type=F32).astype(BF16)
        pk[1, :, cols] = packed
        xs[1, 0:16, cols] = packed[0:16, :]

    def own_chunk(t, c):
        for k in (2 * c, 2 * c + 1):
            if k:
                zc[t][k].wait_recv()
        for y in own[t][c]:
            y.start()

    def pass_on(t, c):
        own[t][c][0 if c < 2 else 1].wait_recv()
        onward[t][c].start()

    def forward(r):
        span = pl.ds(r * rows, rows)
        pre = lax.dot_general(xs[0, span, :], wgu[...], NT, preferred_element_type=F32)
        half = pre.shape[1] // 2
        gate, upper = pre[:, :half], pre[:, half:]
        sig = jax.nn.sigmoid(gate)
        activated = gate * sig
        act[span, :] = activated
        bsl[span, :] = upper * (sig * (1.0 + gate * (1.0 - sig)))
        hid = activated * upper
        hid_t[:, span] = hid.T.astype(BF16)
        hidden = hid.astype(BF16)

        @tiles
        def _(cols):
            part[0, span, cols] = jnp.dot(hidden, wdn[:, cols], preferred_element_type=F32).astype(BF16)

    def backward(r):
        span = pl.ds(r * rows, rows)
        hg = lax.dot_general(xs[1, span, :], wdn[...], NT, preferred_element_type=F32)
        gg, ug = hg * bsl[span, :], hg * act[span, :]
        half = hg.shape[1]
        gr_t[:half, span] = gg.T.astype(BF16)
        gr_t[half:, span] = ug.T.astype(BF16)
        gg, ug = gg.astype(BF16), ug.astype(BF16)

        @tiles
        def _(cols):
            both = jnp.dot(gg, wgu[:half, cols], preferred_element_type=F32)
            both += jnp.dot(ug, wgu[half:, cols], preferred_element_type=F32)
            part[1, span, cols] = both.astype(BF16)

    def send_sums(t):
        for c in (0, 2, 1, 3):
            far[t][c].start()
        for c in range(2):
            near[t][2 + c][0].start()
            near[t][c][1].start()

    def merge(t):
        for c in (0, 2, 1, 3):
            far[t][c].wait_recv()
            r = 1 if c < 2 else 3
            mine, theirs = pl.ds(r * rows + c * 32, 32), pl.ds(c * 32, 32)

            @tiles
            def _(cols):
                total = part[t, mine, cols].astype(F32) + rdiag[t, theirs, cols].astype(F32)
                part[t, mine, cols] = total.astype(BF16)

            near[t][c][0 if c < 2 else 1].start()

    def finish(t, c):
        for y in near[t][c]:
            y.wait_recv()
        span = pl.ds(c * 32, 32)

        @tiles
        def _(cols):
            total = part[t, span, cols].astype(F32) + rown[t, 0, span, cols].astype(F32)
            fin[t, span, cols] = (total + rown[t, 1, span, cols].astype(F32)).astype(BF16)

        for k in (2 * c, 2 * c + 1):
            final[t][k].start()

    own_chunk(0, 0)
    own_chunk(0, 1)
    pass_on(0, 0)
    own_chunk(0, 2)
    pass_on(0, 1)
    own_chunk(0, 3)
    for k in (2, 3, 4, 5, 6, 7, 1):
        zc[1][k].start()
    for m in meta:
        m.start()
    pass_on(0, 2)
    pass_on(0, 3)
    own_chunk(1, 0)
    loads[2].wait()
    loads[3].wait()
    forward(0)
    own_chunk(1, 1)
    own[0][0][1].wait_recv()
    own[0][1][1].wait_recv()
    own[0][2][0].wait_recv()
    own[0][3][0].wait_recv()
    forward(1)
    own_chunk(1, 2)
    pass_on(1, 0)
    forward(3)
    own_chunk(1, 3)
    pass_on(1, 1)
    for c in range(4):
        onward[0][c].wait_recv()
    forward(2)
    send_sums(0)
    pass_on(1, 2)
    pass_on(1, 3)
    backward(0)
    own[1][0][1].wait_recv()
    own[1][1][1].wait_recv()
    own[1][2][0].wait_recv()
    own[1][3][0].wait_recv()
    backward(1)
    merge(0)
    backward(3)
    for c in range(4):
        onward[1][c].wait_recv()
    backward(2)
    send_sums(1)
    for c in range(4):
        finish(0, c)
    merge(1)

    @pl.loop(0, n_tiles)
    def _(j):
        cols = pl.ds(pl.multiple_of(j * COLS, COLS), COLS)
        gdn[:, cols] = jnp.dot(hid_t[...], xs[1, :, cols], preferred_element_type=F32).astype(BF16)

    stores = [
        pltpu.make_async_copy(src, dst, osem.at[i])
        for i, (src, dst) in enumerate(
            ((gdn, gdn_hbm), (ggu, ggu_hbm), (outs.at[0], on_hbm), (outs.at[1], back_hbm))
        )
    ]
    stores[0].start()
    for c in range(4):
        finish(1, c)

    @pl.loop(0, n_tiles)
    def _(j):
        cols = pl.ds(pl.multiple_of(j * COLS, COLS), COLS)
        half = ggu.shape[0] // 2
        for top in (0, half):
            span = pl.ds(top, half)
            ggu[span, cols] = jnp.dot(gr_t[span, :], xs[0, :, cols], preferred_element_type=F32).astype(BF16)

    stores[1].start()

    for t in range(2):
        meta[t].wait_recv()
        there = jnp.broadcast_to(metar[t, 0:1, :], (rows, rows)).T
        pick = jnp.where(there == lane.astype(F32), 1.0, 0.0).astype(BF16)
        scale = jnp.broadcast_to(metar[t, 8:9, :], (rows, rows)).T[:, 0:1]
        edge = s == (0, 7)[t]
        for k in range(8):
            final[t][k].wait_recv()

        @tiles
        def _(cols):
            mixed = jnp.dot(pick, rsec[t, :, cols], preferred_element_type=F32)
            if t == 0:
                mixed = mixed * scale
            outs[t, :, cols] = jnp.where(edge, 0.0, mixed).astype(BF16)

        stores[2 + t].start()

    for c in used:
        c.wait_send()
    for store in stores:
        store.wait()


def shards(tokens, cotangent, routes, gates, gate_up, down):
    rows, width = tokens.shape[1:]
    quarter = down.shape[2]
    both = 2 * quarter
    hbm = pl.BlockSpec(memory_space=pl.ANY)
    vmem = pl.BlockSpec(memory_space=pltpu.VMEM)
    shape = lambda *dims: jax.ShapeDtypeStruct(dims, BF16)
    flops = 2 * 9 * 4 * rows * quarter * width
    on, back, ggu, gdn = pl.pallas_call(
        kernel,
        out_shape=(shape(rows, width), shape(rows, width), shape(both, width), shape(quarter, width)),
        in_specs=[hbm, hbm, vmem, vmem, hbm, hbm],
        out_specs=[hbm] * 4,
        scratch_shapes=[
            pltpu.VMEM((rows, width), BF16),
            pltpu.VMEM((rows, width), BF16),
            pltpu.VMEM((both, width), BF16),
            pltpu.VMEM((quarter, width), BF16),
            pltpu.VMEM((2, rows, width), BF16),
            pltpu.VMEM((2, 4 * rows, width), BF16),
            pltpu.VMEM((2, 4 * rows, width), BF16),
            pltpu.VMEM((2, rows, width), BF16),
            pltpu.VMEM((2, 2, rows, width), BF16),
            pltpu.VMEM((2, rows, width), BF16),
            pltpu.VMEM((2, rows, width), BF16),
            pltpu.VMEM((16, rows), F32),
            pltpu.VMEM((2, 16, rows), F32),
            pltpu.VMEM((4 * rows, quarter), F32),
            pltpu.VMEM((4 * rows, quarter), F32),
            pltpu.VMEM((quarter, 4 * rows), BF16),
            pltpu.VMEM((both, 4 * rows), BF16),
            pltpu.VMEM((both, width), BF16),
            pltpu.VMEM((quarter, width), BF16),
            pltpu.VMEM((2, rows, width), BF16),
            pltpu.SemaphoreType.DMA((4,)),
            pltpu.SemaphoreType.DMA((4,)),
            pltpu.SemaphoreType.DMA((COPIES,)),
            pltpu.SemaphoreType.DMA((COPIES,)),
        ],
        compiler_params=pltpu.CompilerParams(
            collective_id=0, has_side_effects=True, vmem_limit_bytes=56 * 2**20
        ),
        cost_estimate=pl.CostEstimate(flops=flops, bytes_accessed=12 * 2**20, transcendentals=0),
    )(
        tokens[0], cotangent[0], routes[0], gates[0],
        gate_up.reshape(both, width), down.reshape(quarter, width),
    )
    return (
        on[None],
        back[None],
        ggu.reshape(gate_up.shape),
        gdn.reshape(down.shape),
    )


def solution(mesh):
    in_specs = (
        P("section", ("dp", "expert"), None),
        P("section", ("dp", "expert"), None),
        P("section", ("dp", "expert"), None),
        P("section", ("dp", "expert"), None),
        P("section", "expert", None, "dp", None),
        P("section", "expert", "dp", None),
    )
    out_specs = (
        P("section", ("dp", "expert"), None),
        P("section", ("dp", "expert"), None),
        P("section", "expert", None, "dp", None),
        P("section", "expert", "dp", None),
    )
    return jax.shard_map(shards, mesh=mesh, in_specs=in_specs, out_specs=out_specs, check_vma=False)
```

time: 331 us -> 148 us (0.45)
  the two profiles are of different devices: /device:TPU:4 before, /device:TPU:1 now
where the time goes in v1:
time: 148 us
  Pallas kernels  137 us (93%)
  local copies, waits for them, and re-layouts  10.2 us (7%)
    pallas_call x1, Pallas kernels, shards(): pl.pallas_call(kernel, out_shape=(shape(rows, width), shape(rows, width),...  137 us
    unnamed x10, local copies, waits for them, and re-layouts  10.2 us

profile of v1, /device:TPU:1, one launch (start us, length us, event | category | flops | bytes accessed | tf_op | source)
XLA Modules:
  0.0 148.0 jit_solution(12704867200465337312)
XLA Ops:
  0.6 1.4 copy.10
  2.0 1.4 copy.11
  3.5 137.1 %shard_map.93 = (bf16[128,2560]{1,0:T(8,128)(2,1)}, bf16[128,2560]{1,0:T(8,128)(2,1)}, bf16[512,2560]{1,0:T(8,128)(2,1)}, bf16[256,2560]{1,0:T(8,128)(2,1)}) custom-call(bf16[128,2560]{1,0:T(8,128)(2,1)} %bitcast.18, bf16[128,2560]{1,0:T(8,128)(2,1)} %bitcast.19, s32[128,6]{1,0:T(8,128)} %bitcast.14, f32[128,6]{1,0:T(8,128)} %bitcast.15, ...), custom_call_target="tpu_custom_call" | custom-call | flops 6039797760 | bytes 12582912 | tf_op jit(solution)/shard_map/pallas_call | solution.py:342
  140.6 0.0 copy-start
  140.6 2.1 %copy.16 = bf16[1,128,2560]{2,1,0:T(8,128)(2,1)} copy(bf16[1,128,2560]{2,1,0:T(8,128)(2,1)} %bitcast.13) | data formatting | bytes 1310720
  142.7 2.0 %copy.17 = bf16[1,128,2560]{2,1,0:T(8,128)(2,1)} copy(bf16[1,128,2560]{2,1,0:T(8,128)(2,1)} %bitcast.12) | data formatting | bytes 1310720
  144.7 0.0 copy-done
  144.7 0.0 copy-start.1
  144.7 1.5 %copy.18 = bf16[1,1,2,256,2560]{4,3,2,1,0:T(8,128)(2,1)} copy(bf16[1,1,2,256,2560]{4,3,2,1,0:T(8,128)(2,1)S(1)} %bitcast.10) | data formatting | bytes 5242880
  146.1 0.8 copy-done.1
  146.9 1.1 copy.19
Async XLA Ops:
  140.6 4.1 %copy-start = (bf16[512,2560]{1,0:T(8,128)(2,1)S(1)}, bf16[512,2560]{1,0:T(8,128)(2,1)}, u32[]{:S(2)}) copy-start(bf16[512,2560]{1,0:T(8,128)(2,1)} %get-tuple-element.10) | copy-start | bytes 7864324
  144.7 2.3 %copy-start.1 = (bf16[256,2560]{1,0:T(8,128)(2,1)S(1)}, bf16[256,2560]{1,0:T(8,128)(2,1)}, u32[]{:S(2)}) copy-start(bf16[256,2560]{1,0:T(8,128)(2,1)} %get-tuple-element.11) | copy-start | bytes 3932164

commit v2 on v0

v2 whole, which is shorter than its diff:
```python
import functools

import jax
import jax.numpy as jnp
from jax import lax
from jax.experimental import pallas as pl
from jax.experimental.pallas import tpu as pltpu
from jax.sharding import PartitionSpec as P

MESH = pl.DeviceIdType.MESH
F32 = jnp.float32
BF16 = jnp.bfloat16
NT = (((1,), (1,)), ((), ()))
COLS = 512
WIDE = 640
PIECES = ((0,), (1,), (2,), (3,), (4,), (5,), (6,), (7,))
COPIES = 7 + 10 * len(PIECES) + 16 + 2
ORDER = (
    "Z1", "Z2", "Z3", "Z4", "Z5", "Z6", "Z7", "A0", "A1", "B0", "P0", "A2",
    "B1", "C0", "R0", "A3", "M0", "B2", "C1", "R1", "F0", "A4", "M1", "B3",
    "C2", "R2", "F1", "A5", "M2", "B4", "C3", "R3", "F2", "A6", "M3", "B5",
    "C4", "R4", "F3", "A7", "M4", "B6", "C5", "R5", "F4", "M5", "B7", "C6",
    "R6", "F5", "M6", "C7", "R7", "F6", "D0", "M7", "F7", "G0",
)


def flipped(index, bits):
    out = index
    for b in range(3):
        if bits >> b & 1:
            out = out + (1 << b) * (1 - 2 * ((index // (1 << b)) % 2))
    return out


def kernel(
    tok_hbm, cot_hbm, routes_hbm, gates_hbm, gu_hbm, dn_hbm,
    rsec, metar, ggu, gdn,
    tok, cot, wgu, wdn, routes_ref, gates_ref, pk, xs, part, rdiag, rown, fin, metas,
    hid, gr, lsem, ssem, rsem,
):
    s = lax.axis_index("section")
    q = lax.axis_index("dp")
    e = lax.axis_index("expert")
    nxt, prv = (s + 1) % 8, (s + 7) % 8
    up, dwn = (q + 1) % 4, (q + 3) % 4
    rows, width = tok.shape
    quarter = wdn.shape[0]
    left, right = pl.ds(0, width // 2), pl.ds(width // 2, width // 2)

    barrier = pltpu.get_barrier_semaphore()
    peers = [(s, q, flipped(e, k)) for k in range(1, 8)]
    peers += [(s, up, e), (s, dwn, e)]
    peers += [(t, q, flipped(e, k)) for t in (nxt, prv) for k in range(8)]
    for peer in peers:
        pl.semaphore_signal(barrier, inc=1, device_id=peer, device_id_type=MESH)

    loads = [
        pltpu.make_async_copy(src, dst, lsem.at[i])
        for i, (src, dst) in enumerate(
            (
                (tok_hbm, tok), (cot_hbm, cot), (gu_hbm, wgu), (dn_hbm, wdn),
                (routes_hbm, routes_ref), (gates_hbm, gates_ref),
            )
        )
    ]
    for i in (4, 5, 0, 1, 2, 3):
        loads[i].start()
    used = []

    def copy(src, dst, peer):
        i = len(used)
        c = pltpu.make_async_remote_copy(
            src_ref=src, dst_ref=dst, send_sem=ssem.at[i], recv_sem=rsem.at[i],
            device_id=peer, device_id_type=MESH,
        )
        used.append(c)
        return c

    def tiles(body, first=0, last=width, step=COLS):
        @pl.loop(first // step, last // step)
        def _(j):
            body(pl.ds(pl.multiple_of(j * step, step), step))

    start = [64 * sum(len(p) for p in PIECES[:c]) for c in range(len(PIECES))]
    size = [16 * len(p) for p in PIECES]

    def block(r, c):
        return pl.ds(start[c] + r * size[c], size[c])

    def slots(c):
        return pl.ds(16 * PIECES[c][0], size[c])

    both = pl.ds(0, 2)
    zc = {}
    own, onward, far, near, merged, final = [], [], [], [], [], {}
    for c, piece in enumerate(PIECES):
        for i, k in enumerate(piece):
            at = pl.ds(start[c] + 16 * i, 16)
            if k:
                zc[k] = copy(pk.at[both, pl.ds(k * 16, 16)], xs.at[both, at], (s, q, flipped(e, k)))
    for c in range(len(PIECES)):
        own.append([copy(xs.at[both, block(0, c)], xs.at[both, block(r, c)], (s, y, e)) for y, r in ((up, 3), (dwn, 1))])
        onward.append([
            copy(xs.at[both, block(r, c), h], xs.at[both, block(2, c), h], (s, y, e))
            for y, r, h in ((up, 3, left), (dwn, 1, right))
        ])
        far.append([
            copy(part.at[both, block(2, c), h], rdiag.at[both, slots(c), h], (s, y, e))
            for y, h in ((up, left), (dwn, right))
        ])
        near.append([
            copy(part.at[both, block(r, c), h], rown.at[i, both, slots(c), h], (s, y, e))
            for i, (y, r, h) in enumerate(((up, 1, right), (dwn, 3, left)))
        ])
        merged.append([
            copy(part.at[both, block(r, c), h], rown.at[i, both, slots(c), h], (s, y, e))
            for i, (y, r, h) in enumerate(((up, 1, left), (dwn, 3, right)))
        ])
    for t in range(2):
        for k in range(8):
            at = pl.ds(k * 16, 16)
            final[t, k] = copy(fin.at[t, at], rsec.at[t, at], ((nxt, prv)[t], q, flipped(e, k)))
    meta = [copy(metas, metar.at[t], ((nxt, prv)[t], q, e)) for t in range(2)]
    assert len(used) == COPIES

    loads[4].wait()
    loads[5].wait()
    in_window = routes_ref[...] < 8
    expert_of = jnp.sum(jnp.where(in_window, routes_ref[...], 0), 0)
    present = jnp.sum(jnp.where(in_window, 1, 0), 0) > 0
    weight = jnp.sum(jnp.where(in_window, gates_ref[...], 0.0), 0)
    lane = lax.broadcasted_iota(jnp.int32, (rows, rows), 1)
    sub = lax.broadcasted_iota(jnp.int32, (rows, rows), 0)
    member = jnp.where((expert_of == sub[0:16]) & present, 1.0, 0.0)
    earlier = jnp.where(sub < lane, 1.0, 0.0).astype(BF16)
    before = jnp.dot(member.astype(BF16), earlier, preferred_element_type=F32)
    slot = jnp.sum(before * member, 0, keepdims=True)
    column = expert_of ^ e
    place = jnp.where(present, column.astype(F32) * 16.0 + slot, -1.0)
    metas[0:8, :] = jnp.broadcast_to(place, (8, rows))
    metas[8:16, :] = jnp.broadcast_to(weight, (8, rows))
    select = jnp.where(place == sub.astype(F32), 1.0, 0.0).astype(BF16)
    scale_here = jnp.broadcast_to(weight, (rows, rows)).T[:, 0:1]

    for t in range(2):
        loads[t].wait()

        @tiles
        def _(cols):
            values = tok[:, cols] if t == 0 else (cot[:, cols].astype(F32) * scale_here).astype(BF16)
            packed = jnp.dot(select, values, preferred_element_type=F32).astype(BF16)
            pk[t, :, cols] = packed
            xs[t, 0:16, cols] = packed[0:16, :]

    pl.semaphore_wait(barrier, len(peers))

    def send_out(c):
        for k in PIECES[c]:
            if k:
                zc[k].start()

    def spread(c):
        for k in PIECES[c]:
            if k:
                zc[k].wait_recv()
        for y in own[c]:
            y.start()

    def pass_on(c):
        for i in range(2):
            own[c][i].wait_recv()
            onward[c][i].start()

    def compute(c):
        for y in onward[c]:
            y.wait_recv()
        span = pl.ds(start[c], 4 * size[c])
        pre = lax.dot_general(xs[0, span, :], wgu[...], NT, preferred_element_type=F32)
        gate, upper = pre[:, :quarter], pre[:, quarter:]
        sig = jax.nn.sigmoid(gate)
        activated = gate * sig
        hidden = activated * upper
        hid[span, :] = hidden
        hidden = hidden.astype(BF16)
        hg = lax.dot_general(xs[1, span, :], wdn[...], NT, preferred_element_type=F32)
        gg = hg * upper * (sig * (1.0 + gate * (1.0 - sig)))
        ug = hg * activated
        gr[span, :quarter] = gg
        gr[span, quarter:] = ug
        gg, ug = gg.astype(BF16), ug.astype(BF16)

        @tiles
        def _(cols):
            part[0, span, cols] = jnp.dot(hidden, wdn[:, cols], preferred_element_type=F32).astype(BF16)
            into = jnp.dot(gg, wgu[:quarter, cols], preferred_element_type=F32)
            into += jnp.dot(ug, wgu[quarter:, cols], preferred_element_type=F32)
            part[1, span, cols] = into.astype(BF16)

    def reduce(c):
        for y in (*far[c], *near[c]):
            y.start()

    def merge(c):
        for i, (r, first, last) in enumerate(((1, 0, width // 2), (3, width // 2, width))):
            far[c][i].wait_recv()
            mine, theirs = block(r, c), slots(c)

            @functools.partial(tiles, first=first, last=last, step=WIDE)
            def _(cols):
                for t in range(2):
                    total = part[t, mine, cols].astype(F32) + rdiag[t, theirs, cols].astype(F32)
                    part[t, mine, cols] = total.astype(BF16)

            merged[c][i].start()

    def finish(c):
        for y in (*near[c], *merged[c]):
            y.wait_recv()
        mine, span = block(0, c), slots(c)

        @functools.partial(tiles, step=WIDE)
        def _(cols):
            for t in range(2):
                total = part[t, mine, cols].astype(F32) + rown[0, t, span, cols].astype(F32)
                fin[t, span, cols] = (total + rown[1, t, span, cols].astype(F32)).astype(BF16)

        for k in PIECES[c]:
            for t in range(2):
                final[t, k].start()

    def grad_down(_):
        flat = hid[...].T.astype(BF16)

        @tiles
        def _(cols):
            gdn[:, cols] = jnp.dot(flat, xs[1, :, cols], preferred_element_type=F32).astype(BF16)


    def grad_gate_up(_):
        for top in (0, quarter):
            flat = gr[:, top : top + quarter].T.astype(BF16)

            @tiles
            def _(cols):
                ggu[top : top + quarter, cols] = jnp.dot(flat, xs[0, :, cols], preferred_element_type=F32).astype(BF16)


    def ready(_):
        for m in meta:
            m.start()
        for load in loads[2:4]:
            load.wait()

    steps = {
        "Z": send_out, "A": spread, "B": pass_on, "C": compute, "R": reduce, "M": merge, "F": finish,
        "D": grad_down, "G": grad_gate_up, "P": ready,
    }
    for step in ORDER:
        steps[step[0]](int(step[1:]))

    for c in (*meta, *final.values()):
        c.wait_recv()
    for c in used:
        c.wait_send()


def place_rows(slots, metar, ggu, gdn, on_hbm, back_hbm, ggu_hbm, gdn_hbm, outs, sems):
    s = lax.axis_index("section")
    rows, width = on_hbm.shape
    gives = [
        pltpu.make_async_copy(src, dst, sems.at[i])
        for i, (src, dst) in enumerate(
            ((outs.at[0], on_hbm), (outs.at[1], back_hbm), (ggu, ggu_hbm), (gdn, gdn_hbm))
        )
    ]
    for give in gives[2:]:
        give.start()
    lane = lax.broadcasted_iota(jnp.int32, (rows, rows), 1)
    for t in range(2):
        there = jnp.broadcast_to(metar[t, 0:1, :], (rows, rows)).T
        pick = jnp.where(there == lane.astype(F32), 1.0, 0.0).astype(BF16)
        scale = jnp.broadcast_to(metar[t, 8:9, :], (rows, rows)).T[:, 0:1]
        edge = s == (0, 7)[t]

        @pl.loop(0, width // COLS)
        def _(j):
            cols = pl.ds(pl.multiple_of(j * COLS, COLS), COLS)
            mixed = jnp.dot(pick, slots[t, :, cols], preferred_element_type=F32)
            if t == 0:
                mixed = mixed * scale
            outs[t, :, cols] = jnp.where(edge, 0.0, mixed).astype(BF16)

        gives[t].start()
    for give in gives:
        give.wait()


def shards(tokens, cotangent, routes, gates, gate_up, down):
    rows, width = tokens.shape[1:]
    quarter = down.shape[2]
    both = 2 * quarter
    hbm = pl.BlockSpec(memory_space=pl.ANY)
    in_hbm = lambda x: pltpu.with_memory_space_constraint(x, pltpu.HBM)
    vmem = pl.BlockSpec(memory_space=pltpu.VMEM)
    shape = lambda *dims: jax.ShapeDtypeStruct(dims, BF16)
    flops = 2 * 9 * 4 * rows * quarter * width
    handed, metar, ggu, gdn = pl.pallas_call(
        kernel,
        out_shape=(
            pltpu.VMEM((2, rows, width), BF16),
            pltpu.VMEM((2, 16, rows), F32),
            pltpu.VMEM((both, width), BF16),
            pltpu.VMEM((quarter, width), BF16),
        ),
        in_specs=[hbm] * 6,
        out_specs=[vmem] * 4,
        scratch_shapes=[
            pltpu.VMEM((rows, width), BF16),
            pltpu.VMEM((rows, width), BF16),
            pltpu.VMEM((both, width), BF16),
            pltpu.VMEM((quarter, width), BF16),
            pltpu.VMEM((6, 1, rows), jnp.int32),
            pltpu.VMEM((6, 1, rows), F32),
            pltpu.VMEM((2, rows, width), BF16),
            pltpu.VMEM((2, 4 * rows, width), BF16),
            pltpu.VMEM((2, 4 * rows, width), BF16),
            pltpu.VMEM((2, rows, width), BF16),
            pltpu.VMEM((2, 2, rows, width), BF16),
            pltpu.VMEM((2, rows, width), BF16),
            pltpu.VMEM((16, rows), F32),
            pltpu.VMEM((4 * rows, quarter), F32),
            pltpu.VMEM((4 * rows, both), F32),
            pltpu.SemaphoreType.DMA((6,)),
            pltpu.SemaphoreType.DMA((COPIES,)),
            pltpu.SemaphoreType.DMA((COPIES,)),
        ],
        compiler_params=pltpu.CompilerParams(
            collective_id=0, has_side_effects=True, vmem_limit_bytes=40 * 2**20
        ),
        cost_estimate=pl.CostEstimate(flops=flops, bytes_accessed=12 * 2**20, transcendentals=0),
    )(
        in_hbm(tokens[0]), in_hbm(cotangent[0]),
        in_hbm(routes.transpose(2, 0, 1)), in_hbm(gates.transpose(2, 0, 1)),
        in_hbm(gate_up.reshape(both, width)), in_hbm(down.reshape(quarter, width)),
    )
    on, back, ggu, gdn = pl.pallas_call(
        place_rows,
        out_shape=(shape(rows, width), shape(rows, width), shape(both, width), shape(quarter, width)),
        in_specs=[vmem] * 4,
        out_specs=[hbm] * 4,
        scratch_shapes=[pltpu.VMEM((2, rows, width), BF16), pltpu.SemaphoreType.DMA((4,))],
        compiler_params=pltpu.CompilerParams(vmem_limit_bytes=24 * 2**20),
        cost_estimate=pl.CostEstimate(flops=8 * 128 * rows * width, bytes_accessed=11 * 2**20, transcendentals=0),
    )(*(pltpu.with_memory_space_constraint(x, pltpu.VMEM) for x in (handed, metar, ggu, gdn)))
    return (
        on[None],
        back[None],
        ggu.reshape(gate_up.shape),
        gdn.reshape(down.shape),
    )


def solution(mesh):
    in_specs = (
        P("section", ("dp", "expert"), None),
        P("section", ("dp", "expert"), None),
        P("section", ("dp", "expert"), None),
        P("section", ("dp", "expert"), None),
        P("section", "expert", None, "dp", None),
        P("section", "expert", "dp", None),
    )
    out_specs = (
        P("section", ("dp", "expert"), None),
        P("section", ("dp", "expert"), None),
        P("section", "expert", None, "dp", None),
        P("section", "expert", "dp", None),
    )
    return jax.shard_map(shards, mesh=mesh, in_specs=in_specs, out_specs=out_specs, check_vma=False)
```

time: 331 us -> 116 us (0.35)
  the two profiles are of different devices: /device:TPU:4 before, /device:TPU:1 now
where the time goes in v2:
time: 116 us
  Pallas kernels  115 us (99%)
    pallas_call x1, Pallas kernels, shards(): pl.pallas_call(kernel, out_shape=(pltpu.VMEM((2, rows, width), BF16), plt...  112 us
    pallas_call x1, Pallas kernels, shards(): pl.pallas_call(place_rows, out_shape=(shape(rows, width), shape(rows, wid...  2.83 us

profile of v2, /device:TPU:1, one launch (start us, length us, event | category | flops | bytes accessed | tf_op | source)
XLA Modules:
  0.0 115.6 jit_solution(1459947639401112667)
XLA Ops:
  0.6 112.1 %shard_map.93 = (bf16[2,128,2560]{2,1,0:T(8,128)(2,1)S(1)}, f32[2,16,128]{2,1,0:T(8,128)S(1)}, bf16[512,2560]{1,0:T(8,128)(2,1)S(1)}, bf16[256,2560]{1,0:T(8,128)(2,1)S(1)}) custom-call(bf16[128,2560]{1,0:T(8,128)(2,1)} %bitcast.14, bf16[128,2560]{1,0:T(8,128)(2,1)} %bitcast.15, s32[6,1,128]{2,1,0:T(1,128)} %bitcast.18, f32[6,1,128]{2,1,0:T(1,128)} %bitcast.19, ...), custom_call_target="tpu_custom_call" | custom-call | flops 6039797760 | bytes 12582912 | tf_op jit(solution)/shard_map/pallas_call | solution.py:307
  112.8 2.8 %shard_map.94 = (bf16[128,2560]{1,0:T(8,128)(2,1)}, bf16[128,2560]{1,0:T(8,128)(2,1)}, bf16[512,2560]{1,0:T(8,128)(2,1)}, bf16[256,2560]{1,0:T(8,128)(2,1)}) custom-call(bf16[2,128,2560]{2,1,0:T(8,128)(2,1)S(1)} %get-tuple-element.12.slots, f32[2,16,128]{2,1,0:T(8,128)S(1)} %get-tuple-element.13.metar, bf16[512,2560]{1,0:T(8,128)(2,1)S(1)} %get-tuple-element.14.ggu, ...), custom_call_target="tpu_custom_call" | custom-call | flops 335544320 | bytes 11534336 | tf_op jit(solution)/shard_map/pallas_call | solution.py:346

commit v3 on v2

--- a/solution.py
+++ b/solution.py
@@ -17,9 +17,9 @@
 COPIES = 7 + 10 * len(PIECES) + 16 + 2
 ORDER = (
     "Z1", "Z2", "Z3", "Z4", "Z5", "Z6", "Z7", "A0", "A1", "B0", "P0", "A2",
-    "B1", "C0", "R0", "A3", "M0", "B2", "C1", "R1", "F0", "A4", "M1", "B3",
-    "C2", "R2", "F1", "A5", "M2", "B4", "C3", "R3", "F2", "A6", "M3", "B5",
-    "C4", "R4", "F3", "A7", "M4", "B6", "C5", "R5", "F4", "M5", "B7", "C6",
+    "B1", "C0", "R0", "M0", "A3", "B2", "C1", "R1", "F0", "M1", "A4", "B3",
+    "C2", "R2", "F1", "M2", "A5", "B4", "C3", "R3", "F2", "M3", "A6", "B5",
+    "C4", "R4", "F3", "M4", "A7", "B6", "C5", "R5", "F4", "M5", "B7", "C6",
     "R6", "F5", "M6", "C7", "R7", "F6", "D0", "M7", "F7", "G0",
 )
 

time: 116 us -> 115 us (level)
  no operation moved by 1% of the time
where the time goes in v3:
time: 115 us
  Pallas kernels  114 us (99%)
    pallas_call x1, Pallas kernels, shards(): pl.pallas_call(kernel, out_shape=(pltpu.VMEM((2, rows, width), BF16), plt...  112 us
    pallas_call x1, Pallas kernels, shards(): pl.pallas_call(place_rows, out_shape=(shape(rows, width), shape(rows, wid...  2.83 us

profile of v3, /device:TPU:1, one launch (start us, length us, event | category | flops | bytes accessed | tf_op | source)
XLA Modules:
  0.0 115.1 jit_solution(10877325817261315794)
XLA Ops:
  0.6 111.7 %shard_map.93 = (bf16[2,128,2560]{2,1,0:T(8,128)(2,1)S(1)}, f32[2,16,128]{2,1,0:T(8,128)S(1)}, bf16[512,2560]{1,0:T(8,128)(2,1)S(1)}, bf16[256,2560]{1,0:T(8,128)(2,1)S(1)}) custom-call(bf16[128,2560]{1,0:T(8,128)(2,1)} %bitcast.14, bf16[128,2560]{1,0:T(8,128)(2,1)} %bitcast.15, s32[6,1,128]{2,1,0:T(1,128)} %bitcast.18, f32[6,1,128]{2,1,0:T(1,128)} %bitcast.19, ...), custom_call_target="tpu_custom_call" | custom-call | flops 6039797760 | bytes 12582912 | tf_op jit(solution)/shard_map/pallas_call | solution.py:307
  112.3 2.8 %shard_map.94 = (bf16[128,2560]{1,0:T(8,128)(2,1)}, bf16[128,2560]{1,0:T(8,128)(2,1)}, bf16[512,2560]{1,0:T(8,128)(2,1)}, bf16[256,2560]{1,0:T(8,128)(2,1)}) custom-call(bf16[2,128,2560]{2,1,0:T(8,128)(2,1)S(1)} %get-tuple-element.12.slots, f32[2,16,128]{2,1,0:T(8,128)S(1)} %get-tuple-element.13.metar, bf16[512,2560]{1,0:T(8,128)(2,1)S(1)} %get-tuple-element.14.ggu, ...), custom_call_target="tpu_custom_call" | custom-call | flops 335544320 | bytes 11534336 | tf_op jit(solution)/shard_map/pallas_call | solution.py:346

commit v4 on v3

--- a/solution.py
+++ b/solution.py
@@ -20,7 +20,7 @@
     "B1", "C0", "R0", "M0", "A3", "B2", "C1", "R1", "F0", "M1", "A4", "B3",
     "C2", "R2", "F1", "M2", "A5", "B4", "C3", "R3", "F2", "M3", "A6", "B5",
     "C4", "R4", "F3", "M4", "A7", "B6", "C5", "R5", "F4", "M5", "B7", "C6",
-    "R6", "F5", "M6", "C7", "R7", "F6", "D0", "M7", "F7", "G0",
+    "R6", "F5", "M6", "C7", "R7", "F6",  "M7", "F7", "D0", "G0",
 )
 
 

time: 115 us -> 115 us (level)
  no operation moved by 1% of the time
where the time goes in v4:
time: 115 us
  Pallas kernels  114 us (99%)
    pallas_call x1, Pallas kernels, shards(): pl.pallas_call(kernel, out_shape=(pltpu.VMEM((2, rows, width), BF16), plt...  112 us
    pallas_call x1, Pallas kernels, shards(): pl.pallas_call(place_rows, out_shape=(shape(rows, width), shape(rows, wid...  2.83 us

profile of v4, /device:TPU:1, one launch (start us, length us, event | category | flops | bytes accessed | tf_op | source)
XLA Modules:
  0.0 115.1 jit_solution(11724699735472182200)
XLA Ops:
  0.6 111.7 %shard_map.93 = (bf16[2,128,2560]{2,1,0:T(8,128)(2,1)S(1)}, f32[2,16,128]{2,1,0:T(8,128)S(1)}, bf16[512,2560]{1,0:T(8,128)(2,1)S(1)}, bf16[256,2560]{1,0:T(8,128)(2,1)S(1)}) custom-call(bf16[128,2560]{1,0:T(8,128)(2,1)} %bitcast.14, bf16[128,2560]{1,0:T(8,128)(2,1)} %bitcast.15, s32[6,1,128]{2,1,0:T(1,128)} %bitcast.18, f32[6,1,128]{2,1,0:T(1,128)} %bitcast.19, ...), custom_call_target="tpu_custom_call" | custom-call | flops 6039797760 | bytes 12582912 | tf_op jit(solution)/shard_map/pallas_call | solution.py:307
  112.3 2.8 %shard_map.94 = (bf16[128,2560]{1,0:T(8,128)(2,1)}, bf16[128,2560]{1,0:T(8,128)(2,1)}, bf16[512,2560]{1,0:T(8,128)(2,1)}, bf16[256,2560]{1,0:T(8,128)(2,1)}) custom-call(bf16[2,128,2560]{2,1,0:T(8,128)(2,1)S(1)} %get-tuple-element.12.slots, f32[2,16,128]{2,1,0:T(8,128)S(1)} %get-tuple-element.13.metar, bf16[512,2560]{1,0:T(8,128)(2,1)S(1)} %get-tuple-element.14.ggu, ...), custom_call_target="tpu_custom_call" | custom-call | flops 335544320 | bytes 11534336 | tf_op jit(solution)/shard_map/pallas_call | solution.py:346
